TPU v7x, 32 devices: a whole 2x2x4 slice. The times are simulated.
32 devices in a mesh: band: 4 (over x, core), span: 8 (over z, y).
Axes of the slice: x: 2, y: 2, z: 4, core: 2. Of those that a mesh axis runs over, the one named last changes fastest.
Arguments:
- gases: bfloat16 [7, 32, 16384], P(None, None, ('band', 'span')), may hold values from 0 to 1
- pressure_bin: int32 [32, 16384], P(None, ('band', 'span')), may hold values from 0 to 59
- layer_mass: bfloat16 [32, 16384], P(None, ('band', 'span')), may hold values from 0.5 to 2
- cos_zenith: bfloat16 [16384], P(('band', 'span')), may hold values from 0.19921875 to 1
- surface_albedo: bfloat16 [16384], P(('band', 'span')), may hold values from 0.049804688 to 0.8984375
- column_order: int32 [16384], P(('band', 'span')), may hold values from 0 to 511, as said below
- sunlit: int32 [128], P(('band', 'span')), may hold values from 0 to 1, as said below
- absorption: bfloat16 [112, 7, 60], replicated, may hold values from 9.9658966e-05 to 0.099609375
- scattering: bfloat16 [112, 60], replicated, may hold values from 0.19921875 to 0.94921875
Outputs:
- heating: float32 [32, 16384], P(None, ('band', 'span'))
Inputs may be any that keep to these rules, and one draw needn't show every extreme that they name: `column_order`: the 512 entries of each device's slice are a permutation of 0 to 511. The 4 devices with the same index along the second mesh axis hold 8 sunlit blocks together; among them one device has all 4 blocks sunlit and one has none.
All inputs are finite; a program needn't handle non-finite values.
Results may differ from a plain program's by a relative error of at most 0.0003.
Values may be sent and summed in bfloat16 or wider, within the bound.
No kernel may reach another device: no remote copies, remote signals or barrier semaphores. Data moves between devices by JAX's collectives and lax.ppermute only.
A program may use at most 64 MiB of HBM per device.

v0:
```python
import functools
import math

import jax
import jax.numpy as jnp
from jax import lax
from jax.experimental import pallas as pl
from jax.experimental.pallas import tpu as pltpu
from jax.sharding import PartitionSpec as P

LANES = 128
ROWS = 8
TILE = 256
STEP = 4
HALVES = 2
BIN_ROWS = 64
LOG2E = math.log2(math.e)


def invert(x):
    guess = pl.reciprocal(x, approx=True)
    return guess * (2.0 - x * guess)


def heating_kernel(
    per_peer,
    gases_ref,
    bins_ref,
    mass_ref,
    cosine_ref,
    ground_ref,
    order_ref,
    table_ref,
    scatter_ref,
    heat_ref,
    owner_ref,
    gas_buf,
    slope_buf,
    tau_even,
    tau_odd,
    half_even,
    half_odd,
    up_buf,
    rise_buf,
    pass_buf,
    refl_buf,
    fall_buf,
    direct_buf,
    gain_buf,
    net_buf,
):
    gas_count, levels, columns = gases_ref.shape
    points = table_ref.shape[0]
    half = points // HALVES
    vregs = half // ROWS
    groups = levels // STEP
    blocks = columns // LANES
    tiles = columns // TILE

    for gas in range(gas_count):
        gas_buf[gas] = gases_ref[gas].astype(jnp.float32)
    cosine = jnp.broadcast_to(cosine_ref[...].astype(jnp.float32), (ROWS, columns))
    slope_buf[...] = (-LOG2E) / cosine

    def optical(layer, tile, tau_ref, half_ref, slot):
        cols = slice(tile * TILE, (tile + 1) * TILE)
        spread = (BIN_ROWS, TILE)
        bins = jnp.broadcast_to(bins_ref[pl.ds(layer, 1), cols], spread)
        hit = bins == lax.broadcasted_iota(jnp.int32, spread, 0)
        selector = jnp.where(hit, 1.0, 0.0).astype(jnp.bfloat16)
        parts = []
        for gas in range(gas_count):
            amount = jnp.broadcast_to(gas_buf[gas, pl.ds(layer, 1), cols], (16, TILE)).astype(jnp.bfloat16)
            amount = jnp.concatenate([amount] * (BIN_ROWS // 16), axis=0)
            parts.append(amount * selector)
        weighted = jnp.concatenate(parts, axis=0)
        tau_ref[slot, :, cols] = jnp.dot(table_ref[...], weighted, preferred_element_type=jnp.float32)
        half_ref[slot, :, cols] = jnp.dot(scatter_ref[...], selector, preferred_element_type=jnp.float32)

    def advance(first, slots, chunk, tau_ref, half_ref):
        block, part = divmod(chunk, HALVES)
        cols = slice(block * LANES, (block + 1) * LANES)
        rows = slice(part * half, (part + 1) * half)
        shape = (vregs, ROWS, LANES)
        slope = slope_buf[:, cols]
        refl = refl_buf[rows, cols].reshape(shape)
        fall = fall_buf[rows, cols].reshape(shape)
        direct = direct_buf[rows, cols].reshape(shape)
        for slot in range(slots):
            layer = first + slot
            tau = tau_ref[slot, rows, cols].reshape(shape)
            half_albedo = half_ref[slot, rows, cols].reshape(shape)
            fading = jnp.exp2(tau * (-1.66 * LOG2E))
            passed = jnp.exp2(tau * slope)
            reflect = half_albedo * (1.0 - fading)
            transmit = fading + reflect
            below = direct * passed
            source = half_albedo * (direct - below)
            pass_buf[layer, rows, cols] = (1.0 - refl).reshape(half, LANES)
            inverse = invert(1.0 - reflect * refl)
            up = transmit * inverse
            rise = (reflect * fall + source) * inverse
            up_buf[layer, rows, cols] = up.reshape(half, LANES)
            rise_buf[layer, rows, cols] = rise.reshape(half, LANES)
            fall = source + transmit * (fall + refl * rise)
            refl = reflect + transmit * (refl * up)
            direct = below
            gain_buf[part, layer + 1, :, cols] = jnp.sum(direct + fall, axis=0)
        refl_buf[rows, cols] = refl.reshape(half, LANES)
        fall_buf[rows, cols] = fall.reshape(half, LANES)
        direct_buf[rows, cols] = direct.reshape(half, LANES)

    refl_buf[...] = jnp.zeros_like(refl_buf)
    fall_buf[...] = jnp.zeros_like(fall_buf)
    direct_buf[...] = jnp.broadcast_to(cosine[:1], direct_buf.shape)
    for part in range(HALVES):
        gain_buf[part, 0] = cosine * float(vregs)

    work = [(slot, tile) for slot in range(STEP) for tile in range(tiles)]
    for slot, tile in work:
        optical(slot, tile, tau_even, half_even, slot)

    chunks = blocks * HALVES

    def down_pair(pair, carry):
        first = pair * (2 * STEP)
        following = jnp.minimum(first + 2 * STEP, levels - STEP)
        for chunk in range(chunks):
            for slot, tile in work[chunk * len(work) // chunks:(chunk + 1) * len(work) // chunks]:
                optical(first + STEP + slot, tile, tau_odd, half_odd, slot)
            advance(first, STEP, chunk, tau_even, half_even)
        for chunk in range(chunks):
            for slot, tile in work[chunk * len(work) // chunks:(chunk + 1) * len(work) // chunks]:
                optical(following + slot, tile, tau_even, half_even, slot)
            advance(first + STEP, STEP, chunk, tau_odd, half_odd)
        return carry

    lax.fori_loop(0, groups // 2, down_pair, 0)

    ground = jnp.broadcast_to(ground_ref[...].astype(jnp.float32), (ROWS, columns))
    for block in range(blocks):
        cols = slice(block * LANES, (block + 1) * LANES)
        shape = (points // ROWS, ROWS, LANES)
        albedo = ground[:, cols]
        refl = refl_buf[:, cols].reshape(shape)
        arriving = (fall_buf[:, cols] + direct_buf[:, cols]).reshape(shape)
        rising = albedo * arriving / (1.0 - albedo * refl)
        fall_buf[:, cols] = rising.reshape(points, LANES)
        taken = jnp.sum(rising * (1.0 - refl), axis=0)
        total = gain_buf[0, levels, :, cols]
        for part in range(1, HALVES):
            total = total + gain_buf[part, levels, :, cols]
        net_buf[levels, :, cols] = total - taken

    def up_group(index, carry):
        last = levels - 1 - index * STEP
        for block in range(blocks):
            cols = slice(block * LANES, (block + 1) * LANES)
            shape = (points // ROWS, ROWS, LANES)
            rising = fall_buf[:, cols].reshape(shape)
            for slot in range(STEP):
                layer = last - slot
                rising = up_buf[layer, :, cols].reshape(shape) * rising + rise_buf[layer, :, cols].reshape(shape)
                taken = jnp.sum(rising * pass_buf[layer, :, cols].reshape(shape), axis=0)
                total = gain_buf[0, layer, :, cols]
                for part in range(1, HALVES):
                    total = total + gain_buf[part, layer, :, cols]
                net_buf[layer, :, cols] = total - taken
            fall_buf[:, cols] = rising.reshape(points, LANES)
        return carry

    lax.fori_loop(0, groups, up_group, 0)

    heat = jnp.sum(net_buf[:levels] - net_buf[1:], axis=1)
    heat_ref[...] = heat / mass_ref[...].astype(jnp.float32)

    spread = (columns, columns)
    order = jnp.broadcast_to(order_ref[...], spread)
    match = jnp.where(order == lax.broadcasted_iota(jnp.int32, spread, 0), 1.0, 0.0).astype(jnp.bfloat16)
    place = lax.broadcasted_iota(jnp.int32, (ROWS, columns), 1)
    group = (place // per_peer).astype(jnp.float32).astype(jnp.bfloat16)
    owner = lax.dot_general(group, match, (((1,), (1,)), ((), ())), preferred_element_type=jnp.float32)
    owner_ref[...] = owner.astype(jnp.int32)


def local(
    gases,
    pressure_bin,
    layer_mass,
    cos_zenith,
    surface_albedo,
    column_order,
    sunlit,
    absorption,
    scattering,
):
    group_size = lax.axis_size("span")
    me = lax.axis_index("span")
    gas_count, levels, columns = gases.shape
    points, _, bins = absorption.shape
    table = jnp.pad(absorption, ((0, 0), (0, 0), (0, BIN_ROWS - bins))).reshape(points, gas_count * BIN_ROWS)
    scatter = jnp.pad(0.5 * scattering, ((0, 0), (0, BIN_ROWS - bins)))
    flags = lax.all_gather(sunlit, "span", axis=0, tiled=False)
    field = pltpu.VMEM((levels, points, columns), jnp.float32)
    staged = pltpu.VMEM((STEP, points, columns), jnp.float32)
    state = pltpu.VMEM((points, columns), jnp.float32)
    heat, owner = pl.pallas_call(
        functools.partial(heating_kernel, columns // group_size),
        out_shape=(
            jax.ShapeDtypeStruct((levels, columns), jnp.float32),
            jax.ShapeDtypeStruct((ROWS, columns), jnp.int32),
        ),
        in_specs=[pl.BlockSpec(memory_space=pltpu.VMEM)] * 8,
        out_specs=(pl.BlockSpec(memory_space=pltpu.VMEM),) * 2,
        scratch_shapes=[
            pltpu.VMEM(gases.shape, jnp.float32),
            pltpu.VMEM((ROWS, columns), jnp.float32),
            staged,
            staged,
            staged,
            staged,
            field,
            field,
            field,
            state,
            state,
            state,
            pltpu.VMEM((HALVES, levels + 1, ROWS, columns), jnp.float32),
            pltpu.VMEM((levels + 1, ROWS, columns), jnp.float32),
        ],
        compiler_params=pltpu.CompilerParams(vmem_limit_bytes=48 * 1024 * 1024),
    )(
        gases,
        pressure_bin,
        layer_mass,
        cos_zenith.reshape(1, columns),
        surface_albedo.reshape(1, columns),
        column_order.reshape(1, columns),
        table,
        scatter,
    )
    per_peer = columns // group_size
    block_cols = columns // sunlit.shape[0]
    mine = lax.dynamic_index_in_dim(flags, me * per_peer // block_cols, axis=1, keepdims=False)
    lit = jnp.sum(jnp.where(owner[0][None] == jnp.arange(group_size, dtype=jnp.int32)[:, None], mine[:, None], 0), axis=0)
    return heat * lit.astype(jnp.float32)


def solution(mesh):
    placed = (
        P(None, None, ("band", "span")),
        P(None, ("band", "span")),
        P(None, ("band", "span")),
        P(("band", "span")),
        P(("band", "span")),
        P(("band", "span")),
        P(("band", "span")),
        P(),
        P(),
    )
    return jax.shard_map(
        local, mesh=mesh, in_specs=placed, out_specs=P(None, ("band", "span")), check_vma=False
    )
```

profile of v0, /device:TPU:0, one launch (start us, length us, event | category | flops | bytes accessed | tf_op | source)
XLA Modules:
  0.0 33.5 jit_solution(3043254272551068323)
XLA Ops:
  0.0 0.0 copy-start.8
  0.0 0.7 %copy-done.8 = u32[32]{0:T(128)S(1)} copy-done((u32[32]{0:T(128)S(1)}, u32[32]{0:T(128)}, u32[]{:S(2)}) %copy-start.8) | copy-done | bytes 152
  0.7 0.6 %dynamic-slice = u32[1]{0:T(128)} dynamic-slice(u32[32]{0:T(128)S(1)} %copy-done.8, u32[]{:T(128)S(6)} %add.10), dynamic_slice_sizes={1} | dynamic-slice | bytes 12
  1.9 0.0 copy-start.7
  1.9 0.6 %copy-done.7 = s32[4]{0:T(128)S(1)} copy-done((s32[4]{0:T(128)S(1)}, s32[4]{0:T(128)}, u32[]{:S(2)}) %copy-start.7) | copy-done | bytes 40
  2.5 0.2 dynamic-update-slice
  2.7 0.1 reshape.19
  2.8 13.1 %all-reduce.3 = s32[8,4]{1,0:T(8,128)S(1)} all-reduce(s32[8,4]{1,0:T(8,128)S(1)} %reshape.19), channel_id=2, replica_groups=mesh['band'=4,'span'=8] {'span'}, use_global_device_ids=true, to_apply=%add.2 | all-reduce | flops 32 | bytes 256
  15.9 0.2 dynamic-slice_reduce_fusion
  16.1 0.0 copy-start.4
  16.1 0.9 %pad.8 = bf16[112,7,64]{0,2,1:T(8,128)(2,1)S(1)} pad(bf16[112,7,60]{0,2,1:T(8,128)(2,1)} %param.16, bf16[]{:T(256)} %constant.22.clone.1), padding=0_0x0_0x0_4 | pad | bytes 194434 | tf_op jit(solution)/shard_map/jit(_pad)/pad | solution.py:201
  17.0 0.0 copy-start
  17.0 0.1 copy.18.table_ref
  17.1 0.0 copy-done.4
  17.1 0.1 copy.16
  17.3 0.0 copy-start.1
  17.3 0.0 copy-start.5
  17.3 0.0 copy-start.2
  17.3 0.7 %copy-done.5 = bf16[512]{0:T(512)(128)(2,1)S(1)} copy-done((bf16[512]{0:T(512)(128)(2,1)S(1)}, bf16[512]{0:T(512)(128)(2,1)}, u32[]{:S(2)}) %copy-start.5) | copy-done | bytes 1048
  18.0 0.0 copy-start.6
  18.0 0.7 %copy-done.6 = bf16[512]{0:T(512)(128)(2,1)S(1)} copy-done((bf16[512]{0:T(512)(128)(2,1)S(1)}, bf16[512]{0:T(512)(128)(2,1)}, u32[]{:S(2)}) %copy-start.6) | copy-done | bytes 1048
  18.7 0.0 copy-start.3
  18.7 0.0 copy-done
  18.7 0.0 copy-done.1
  18.7 0.0 copy-done.2
  18.7 0.7 %copy-done.3 = s32[512]{0:T(512)S(1)} copy-done((s32[512]{0:T(512)S(1)}, s32[512]{0:T(512)}, u32[]{:S(2)}) %copy-start.3) | copy-done | bytes 2072
  19.4 13.4 %shard_map.91 = (f32[32,512]{1,0:T(8,128)S(1)}, s32[8,512]{1,0:T(8,128)S(1)}) custom-call(bf16[7,32,512]{2,1,0:T(8,128)(2,1)S(1)} %copy-done, s32[32,512]{1,0:T(8,128)S(1)} %copy-done.1, bf16[32,512]{1,0:T(8,128)(2,1)S(1)} %copy-done.2, bf16[1,512]{1,0:T(2,128)(2,1)S(1)} %reshape.15.cosine_ref, bf16[1,512]{1,0:T(2,128)(2,1)S(1)} %reshape.16.ground_ref, ...), custom_call_target="tpu_custom_call" | custom-call | tf_op jit(solution)/shard_map/pallas_call | solution.py:207
  32.7 0.1 select_reduce_fusion
  32.8 0.7 %broadcast_multiply_fusion = f32[32,512]{1,0:T(8,128)} fusion(f32[32,512]{1,0:T(8,128)S(1)} %get-tuple-element.7, f32[512]{0:T(512)S(1)} %convert_element_type.11), kind=kLoop, calls=%fused_computation | loop fusion | flops 16384 | bytes 133120 | tf_op jit(solution)/shard_map/mul | solution.py:246
  (7 shorter events, 0.0 us)
Async XLA Ops:
  0.0 0.7 %copy-start.8 = (u32[32]{0:T(128)S(1)}, u32[32]{0:T(128)}, u32[]{:S(2)}) copy-start(u32[32]{0:T(128)} %constant.39) | copy-start | bytes 388
  1.9 0.7 %copy-start.7 = (s32[4]{0:T(128)S(1)}, s32[4]{0:T(128)}, u32[]{:S(2)}) copy-start(s32[4]{0:T(128)} %param.15) | copy-start | bytes 52
  16.1 1.1 %copy-start.4 = (bf16[112,60]{0,1:T(8,128)(2,1)S(1)}, bf16[112,60]{0,1:T(8,128)(2,1)}, u32[]{:S(2)}) copy-start(bf16[112,60]{0,1:T(8,128)(2,1)} %param.17) | copy-start | bytes 40324
  17.0 1.7 %copy-start = (bf16[7,32,512]{2,1,0:T(8,128)(2,1)S(1)}, bf16[7,32,512]{2,1,0:T(8,128)(2,1)}, u32[]{:S(2)}) copy-start(bf16[7,32,512]{2,1,0:T(8,128)(2,1)} %gases_ref.1) | copy-start | bytes 688132
  17.3 1.4 %copy-start.1 = (s32[32,512]{1,0:T(8,128)S(1)}, s32[32,512]{1,0:T(8,128)}, u32[]{:S(2)}) copy-start(s32[32,512]{1,0:T(8,128)} %bins_ref.1) | copy-start | bytes 196612
  17.3 0.7 %copy-start.5 = (bf16[512]{0:T(512)(128)(2,1)S(1)}, bf16[512]{0:T(512)(128)(2,1)}, u32[]{:S(2)}) copy-start(bf16[512]{0:T(512)(128)(2,1)} %param.12) | copy-start | bytes 3076
  17.3 1.4 %copy-start.2 = (bf16[32,512]{1,0:T(8,128)(2,1)S(1)}, bf16[32,512]{1,0:T(8,128)(2,1)}, u32[]{:S(2)}) copy-start(bf16[32,512]{1,0:T(8,128)(2,1)} %mass_ref.1) | copy-start | bytes 98308
  18.0 0.7 %copy-start.6 = (bf16[512]{0:T(512)(128)(2,1)S(1)}, bf16[512]{0:T(512)(128)(2,1)}, u32[]{:S(2)}) copy-start(bf16[512]{0:T(512)(128)(2,1)} %param.13) | copy-start | bytes 3076
  18.7 0.7 %copy-start.3 = (s32[512]{0:T(512)S(1)}, s32[512]{0:T(512)}, u32[]{:S(2)}) copy-start(s32[512]{0:T(512)} %param.14) | copy-start | bytes 6148
where the time goes:
time: 33.7 us; the launch traced here: 33.5 us
  Pallas kernels  13.4 us (40%)
  blocking collectives  13.1 us (39%)
  local copies, waits for them, and re-layouts  5.53 us (16%)
  between operations  0.76 us (2%)
  other arithmetic  0.75 us (2%)
    pallas_call x1, Pallas kernels, local(): pl.pallas_call(functools.partial(heating_kernel, columns // group_size),...  13.4 us
    unnamed x1, blocking collectives  13.1 us
    unnamed x22, local copies, waits for them, and re-layouts  4.2 us
    pad x1, local copies, waits for them, and re-layouts, local(): jnp.pad(absorption, ((0, 0), (0, 0), (0, BIN_ROWS - bins)))  0.94 us

commit v1 on v0

--- a/solution.py
+++ b/solution.py
@@ -18,22 +18,33 @@
 
 
 def invert(x):
-    guess = pl.reciprocal(x, approx=True)
-    return guess * (2.0 - x * guess)
+    return pl.reciprocal(x, approx=True)
 
 
 def heating_kernel(
     per_peer,
+    gases_hbm,
+    bins_hbm,
+    mass_hbm,
+    cosine_hbm,
+    ground_hbm,
+    order_hbm,
+    absorb_hbm,
+    scatter_hbm,
+    heat_ref,
+    owner_ref,
     gases_ref,
     bins_ref,
     mass_ref,
     cosine_ref,
     ground_ref,
     order_ref,
+    absorb_ref,
+    albedo_ref,
+    copied,
+    wide_buf,
     table_ref,
     scatter_ref,
-    heat_ref,
-    owner_ref,
     gas_buf,
     slope_buf,
     tau_even,
@@ -57,9 +68,43 @@
     blocks = columns // LANES
     tiles = columns // TILE
 
+    copies = [
+        pltpu.make_async_copy(source, target, copied.at[place])
+        for place, (source, target) in enumerate(
+            (
+                (absorb_hbm, absorb_ref),
+                (scatter_hbm, albedo_ref),
+                (cosine_hbm, cosine_ref),
+                (bins_hbm, bins_ref),
+                (gases_hbm, gases_ref),
+                (ground_hbm, ground_ref),
+                (order_hbm, order_ref),
+                (mass_hbm, mass_ref),
+            )
+        )
+    ]
+    for copy in copies:
+        copy.start()
+    refl_buf[...] = jnp.zeros_like(refl_buf)
+    fall_buf[...] = jnp.zeros_like(fall_buf)
+    wide_buf[...] = jnp.zeros_like(wide_buf)
+    for copy in copies:
+        copy.wait()
+
+    for gas in range(gas_count):
+        wide_buf[gas * BIN_ROWS : gas * BIN_ROWS + absorb_ref.shape[1], :points] = absorb_ref[gas].astype(jnp.float32)
+    first_row = gas_count * BIN_ROWS
+    wide_buf[first_row : first_row + absorb_ref.shape[1], :points] = 0.5 * albedo_ref[...].astype(jnp.float32)
+    turned = [
+        jnp.transpose(wide_buf[i * LANES : (i + 1) * LANES])[:points].astype(jnp.bfloat16)
+        for i in range(wide_buf.shape[0] // LANES)
+    ]
+    whole = jnp.concatenate(turned, axis=1)
+    table_ref[...] = whole[:, :first_row]
+    scatter_ref[...] = whole[:, first_row : first_row + BIN_ROWS]
     for gas in range(gas_count):
         gas_buf[gas] = gases_ref[gas].astype(jnp.float32)
-    cosine = jnp.broadcast_to(cosine_ref[...].astype(jnp.float32), (ROWS, columns))
+    cosine = jnp.broadcast_to(cosine_ref[...].astype(jnp.float32).reshape(1, columns), (ROWS, columns))
     slope_buf[...] = (-LOG2E) / cosine
 
     def optical(layer, tile, tau_ref, half_ref, slot):
@@ -110,8 +155,6 @@
         fall_buf[rows, cols] = fall.reshape(half, LANES)
         direct_buf[rows, cols] = direct.reshape(half, LANES)
 
-    refl_buf[...] = jnp.zeros_like(refl_buf)
-    fall_buf[...] = jnp.zeros_like(fall_buf)
     direct_buf[...] = jnp.broadcast_to(cosine[:1], direct_buf.shape)
     for part in range(HALVES):
         gain_buf[part, 0] = cosine * float(vregs)
@@ -137,7 +180,7 @@
 
     lax.fori_loop(0, groups // 2, down_pair, 0)
 
-    ground = jnp.broadcast_to(ground_ref[...].astype(jnp.float32), (ROWS, columns))
+    ground = jnp.broadcast_to(ground_ref[...].astype(jnp.float32).reshape(1, columns), (ROWS, columns))
     for block in range(blocks):
         cols = slice(block * LANES, (block + 1) * LANES)
         shape = (points // ROWS, ROWS, LANES)
@@ -198,9 +241,10 @@
     me = lax.axis_index("span")
     gas_count, levels, columns = gases.shape
     points, _, bins = absorption.shape
-    table = jnp.pad(absorption, ((0, 0), (0, 0), (0, BIN_ROWS - bins))).reshape(points, gas_count * BIN_ROWS)
-    scatter = jnp.pad(0.5 * scattering, ((0, 0), (0, BIN_ROWS - bins)))
-    flags = lax.all_gather(sunlit, "span", axis=0, tiled=False)
+    ring = [
+        lax.ppermute(sunlit, "span", [(i, (i + hop) % group_size) for i in range(group_size)])
+        for hop in range(1, group_size)
+    ]
     field = pltpu.VMEM((levels, points, columns), jnp.float32)
     staged = pltpu.VMEM((STEP, points, columns), jnp.float32)
     state = pltpu.VMEM((points, columns), jnp.float32)
@@ -210,9 +254,21 @@
             jax.ShapeDtypeStruct((levels, columns), jnp.float32),
             jax.ShapeDtypeStruct((ROWS, columns), jnp.int32),
         ),
-        in_specs=[pl.BlockSpec(memory_space=pltpu.VMEM)] * 8,
+        in_specs=[pl.BlockSpec(memory_space=pltpu.HBM)] * 8,
         out_specs=(pl.BlockSpec(memory_space=pltpu.VMEM),) * 2,
         scratch_shapes=[
+            pltpu.VMEM(gases.shape, gases.dtype),
+            pltpu.VMEM(pressure_bin.shape, pressure_bin.dtype),
+            pltpu.VMEM(layer_mass.shape, layer_mass.dtype),
+            pltpu.VMEM(cos_zenith.shape, cos_zenith.dtype),
+            pltpu.VMEM(surface_albedo.shape, surface_albedo.dtype),
+            pltpu.VMEM((1, columns), column_order.dtype),
+            pltpu.VMEM((gas_count, bins, points), absorption.dtype),
+            pltpu.VMEM((bins, points), scattering.dtype),
+            pltpu.SemaphoreType.DMA((8,)),
+            pltpu.VMEM((-(-(gas_count + 1) * BIN_ROWS // LANES) * LANES, LANES), jnp.float32),
+            pltpu.VMEM((points, gas_count * BIN_ROWS), jnp.bfloat16),
+            pltpu.VMEM((points, BIN_ROWS), jnp.bfloat16),
             pltpu.VMEM(gases.shape, jnp.float32),
             pltpu.VMEM((ROWS, columns), jnp.float32),
             staged,
@@ -229,20 +285,23 @@
             pltpu.VMEM((levels + 1, ROWS, columns), jnp.float32),
         ],
         compiler_params=pltpu.CompilerParams(vmem_limit_bytes=48 * 1024 * 1024),
+        cost_estimate=pl.CostEstimate(
+            flops=40 * levels * points * columns, bytes_accessed=1 << 20, transcendentals=3 * levels * points * columns
+        ),
     )(
         gases,
         pressure_bin,
         layer_mass,
-        cos_zenith.reshape(1, columns),
-        surface_albedo.reshape(1, columns),
+        cos_zenith,
+        surface_albedo,
         column_order.reshape(1, columns),
-        table,
-        scatter,
+        jnp.transpose(absorption, (1, 2, 0)),
+        jnp.transpose(scattering),
     )
-    per_peer = columns // group_size
-    block_cols = columns // sunlit.shape[0]
-    mine = lax.dynamic_index_in_dim(flags, me * per_peer // block_cols, axis=1, keepdims=False)
-    lit = jnp.sum(jnp.where(owner[0][None] == jnp.arange(group_size, dtype=jnp.int32)[:, None], mine[:, None], 0), axis=0)
+    place = me * (columns // group_size) // (columns // sunlit.shape[0])
+    flags = lax.dynamic_index_in_dim(jnp.stack([sunlit] + ring), place, axis=1, keepdims=False)
+    hops = lax.rem(me - owner[0] + group_size, group_size)
+    lit = jnp.sum(jnp.where(hops[None] == jnp.arange(group_size, dtype=jnp.int32)[:, None], flags[:, None], 0), axis=0)
     return heat * lit.astype(jnp.float32)
 
 

time: 33.7 us -> 37 us (1.098)
  starting transfers between devices: 0 us -> 14.2 us
  blocking collectives: 13.1 us -> 0 us
  waiting for transfers between devices: 0 us -> 3.52 us
  between operations: 0.76 us -> 0.08 us
  local copies, waits for them, and re-layouts: 5.53 us -> 4.94 us
    ppermute x0 -> x7, starting transfers between devices: none -> 14.2 us  [local(): lax.ppermute(sunlit, 'span', [(i, (i + hop) % group_size) for i in range(...]
    unnamed x1 -> x0, blocking collectives: 13.1 us -> none
    ppermute x0 -> x7, waiting for transfers between devices: none -> 3.52 us  [local(): lax.ppermute(sunlit, 'span', [(i, (i + hop) % group_size) for i in range(...]
    pad x2 -> x0, local copies, waits for them, and re-layouts: 0.95 us -> none  [the longest x1 0.94 us: local(): jnp.pad(absorption, ((0, 0), (0, 0), (0, BIN_ROWS - bins)))]
    unnamed x22 -> x18, local copies, waits for them, and re-layouts: 4.2 us -> 4.73 us
  transfers between devices with their start and end apart: 0 -> 7, of which waited for: 0 -> 2; matrix products, arithmetic and copies ran while one was open for 0% -> 0% of each run, Pallas kernels for 0% -> 36%
where the time goes in v1:
time: 37 us; the launch traced here: 36.7 us
  starting transfers between devices  14.2 us (38%)
  Pallas kernels  13.3 us (36%)
  local copies, waits for them, and re-layouts  4.94 us (13%)
  waiting for transfers between devices  3.52 us (10%)
  other arithmetic  0.75 us (2%)
    ppermute x7, starting transfers between devices, local(): lax.ppermute(sunlit, 'span', [(i, (i + hop) % group_size) for i in range(...  14.2 us
    pallas_call x1, Pallas kernels, local(): pl.pallas_call(functools.partial(heating_kernel, columns // group_size),...  13.3 us
    unnamed x18, local copies, waits for them, and re-layouts  4.73 us
    ppermute x7, waiting for transfers between devices, local(): lax.ppermute(sunlit, 'span', [(i, (i + hop) % group_size) for i in range(...  3.52 us
  transfers between devices with their start and end apart: 7, of which 2 were waited for; matrix products, arithmetic and copies ran while one was open for 0% of the time, Pallas kernels for 36%

profile of v1, /device:TPU:0, one launch (start us, length us, event | category | flops | bytes accessed | tf_op | source)
XLA Modules:
  0.0 36.7 jit_solution(12516479473702150598)
XLA Ops:
  0.0 0.0 copy-start.3
  0.0 5.0 %collective-permute-start.4 = (s32[4]{0:T(128)}, s32[4]{0:T(128)S(1)}, u32[]{:S(2)}, u32[]{:S(2)}) collective-permute-start(s32[4]{0:T(128)} %param.15), channel_id=1, source_target_pairs={{0,5},{1,6},{2,7},{3,0},{4,1},{5,2},{6,3},{7,4},{8,13},{9,14},{10,... | collective-permute-start | bytes 56 | tf_op jit(solution)/shard_map/ppermute | solution.py:245
  5.0 0.3 collective-permute-start.3
  5.3 1.6 %collective-permute-start.2 = (s32[4]{0:T(128)}, s32[4]{0:T(128)S(1)}, u32[]{:S(2)}, u32[]{:S(2)}) collective-permute-start(s32[4]{0:T(128)} %param.15), channel_id=1, source_target_pairs={{0,3},{1,4},{2,5},{3,6},{4,7},{5,0},{6,1},{7,2},{8,11},{9,12},{10,... | collective-permute-start | bytes 56 | tf_op jit(solution)/shard_map/ppermute | solution.py:245
  7.0 2.5 %collective-permute-start.1 = (s32[4]{0:T(128)}, s32[4]{0:T(128)S(1)}, u32[]{:S(2)}, u32[]{:S(2)}) collective-permute-start(s32[4]{0:T(128)} %param.15), channel_id=1, source_target_pairs={{0,2},{1,3},{2,4},{3,5},{4,6},{5,7},{6,0},{7,1},{8,10},{9,11},{10,... | collective-permute-start | bytes 56 | tf_op jit(solution)/shard_map/ppermute | solution.py:245
  9.4 1.5 %collective-permute-start = (s32[4]{0:T(128)}, s32[4]{0:T(128)S(1)}, u32[]{:S(2)}, u32[]{:S(2)}) collective-permute-start(s32[4]{0:T(128)} %param.15), channel_id=1, source_target_pairs={{0,1},{1,2},{2,3},{3,4},{4,5},{5,6},{6,7},{7,0},{8,9},{9,10},{10,1... | collective-permute-start | bytes 56 | tf_op jit(solution)/shard_map/ppermute | solution.py:245
  11.0 0.0 copy-start.7
  11.0 0.0 copy-start.5
  11.0 0.0 copy-start.6
  11.0 0.0 copy-done.3
  11.0 0.7 %copy-done.7 = bf16[512]{0:T(512)(128)(2,1)S(1)} copy-done((bf16[512]{0:T(512)(128)(2,1)S(1)}, bf16[512]{0:T(512)(128)(2,1)}, u32[]{:S(2)}) %copy-start.7) | copy-done | bytes 1048
  11.6 0.0 copy-done.5
  11.7 0.0 copy-done.6
  11.7 0.0 copy-start
  11.7 0.9 %copy-done = bf16[7,32,512]{2,1,0:T(8,128)(2,1)S(1)} copy-done((bf16[7,32,512]{2,1,0:T(8,128)(2,1)S(1)}, bf16[7,32,512]{2,1,0:T(8,128)(2,1)}, u32[]{:S(2)}) %copy-start) | copy-done | bytes 229400
  12.6 0.0 copy-start.1
  12.6 0.9 %copy-done.1 = bf16[112,7,60]{0,2,1:T(8,128)(2,1)S(1)} copy-done((bf16[112,7,60]{0,2,1:T(8,128)(2,1)S(1)}, bf16[112,7,60]{0,2,1:T(8,128)(2,1)}, u32[]{:S(2)}) %copy-start.1) | copy-done | bytes 94104
  13.5 0.0 copy-start.2
  13.5 0.8 %copy-done.2 = s32[32,512]{1,0:T(8,128)S(1)} copy-done((s32[32,512]{1,0:T(8,128)S(1)}, s32[32,512]{1,0:T(8,128)}, u32[]{:S(2)}) %copy-start.2) | copy-done | bytes 65560
  14.3 0.0 copy-start.4
  14.4 0.7 %copy-done.4 = bf16[112,60]{0,1:T(8,128)(2,1)S(1)} copy-done((bf16[112,60]{0,1:T(8,128)(2,1)S(1)}, bf16[112,60]{0,1:T(8,128)(2,1)}, u32[]{:S(2)}) %copy-start.4) | copy-done | bytes 13464
  15.1 13.3 %shard_map.91 = (f32[32,512]{1,0:T(8,128)S(1)}, s32[8,512]{1,0:T(8,128)S(1)}) custom-call(bf16[7,32,512]{2,1,0:T(8,128)(2,1)S(1)} %copy-done, s32[32,512]{1,0:T(8,128)S(1)} %copy-done.2, bf16[32,512]{1,0:T(8,128)(2,1)S(1)} %copy-done.3, bf16[512]{0:T(512)(128)(2,1)S(1)} %copy-done.6, bf16[512]{0:T(512)(128)(2,1)S(1)} %copy-done.7, s32[1,512]{1,0:T(1,128)S(1)} %bitcast.14, ...), custom_call_target="tpu_custom_call" | custom-call | flops 73400320 | bytes 1048576 | tf_op jit(solution)/shard_map/pallas_call | solution.py:251
  28.4 0.0 copy-start.8
  28.4 0.0 collective-permute-done.4
  28.4 0.6 %copy-done.8 = s32[4]{0:T(128)S(1)} copy-done((s32[4]{0:T(128)S(1)}, s32[4]{0:T(128)}, u32[]{:S(2)}) %copy-start.8) | copy-done | bytes 40
  29.0 3.2 %collective-permute-start.6 = (s32[4]{0:T(128)S(1)}, s32[4]{0:T(128)S(1)}, u32[]{:S(2)}, u32[]{:S(2)}) collective-permute-start(s32[4]{0:T(128)S(1)} %copy-done.8), channel_id=1, source_target_pairs={{0,7},{1,0},{2,1},{3,2},{4,3},{5,4},{6,5},{7,6},{8,15},{9,8},{10,9... | collective-permute-start | bytes 56 | tf_op jit(solution)/shard_map/ppermute | solution.py:245
  32.3 0.0 collective-permute-done.3
  32.3 0.0 collective-permute-start.5
  32.3 0.0 collective-permute-done.2
  32.3 0.0 collective-permute-done.1
  32.3 0.0 collective-permute-done
  32.3 1.3 %collective-permute-done.6 = s32[4]{0:T(128)S(1)} collective-permute-done((s32[4]{0:T(128)S(1)}, s32[4]{0:T(128)S(1)}, u32[]{:S(2)}, u32[]{:S(2)}) %collective-permute-start.6) | collective-permute-done | bytes 48 | tf_op jit(solution)/shard_map/ppermute | solution.py:245
  33.5 2.2 %collective-permute-done.5 = s32[4]{0:T(128)S(1)} collective-permute-done((s32[4]{0:T(128)S(1)}, s32[4]{0:T(128)S(1)}, u32[]{:S(2)}, u32[]{:S(2)}) %collective-permute-start.5) | collective-permute-done | bytes 48 | tf_op jit(solution)/shard_map/ppermute | solution.py:245
  35.8 0.2 dynamic-slice_reduce_fusion
  36.0 0.1 select_reduce_fusion
  36.1 0.6 %broadcast_multiply_fusion = f32[32,512]{1,0:T(8,128)} fusion(f32[32,512]{1,0:T(8,128)S(1)} %get-tuple-element.7, f32[512]{0:T(512)S(1)} %convert_element_type.7), kind=kLoop, calls=%fused_computation | loop fusion | flops 16384 | bytes 133120 | tf_op jit(solution)/shard_map/mul | solution.py:305
  (3 shorter events, 0.0 us)
Async XLA Ops:
  0.0 11.0 %copy-start.3 = (bf16[32,512]{1,0:T(8,128)(2,1)S(1)}, bf16[32,512]{1,0:T(8,128)(2,1)}, u32[]{:S(2)}) copy-start(bf16[32,512]{1,0:T(8,128)(2,1)} %mass_hbm.1) | copy-start | bytes 98308
  0.0 28.4 %collective-permute-start.4 = (s32[4]{0:T(128)}, s32[4]{0:T(128)S(1)}, u32[]{:S(2)}, u32[]{:S(2)}) collective-permute-start(s32[4]{0:T(128)} %param.15), channel_id=1, source_target_pairs={{0,5},{1,6},{2,7},{3,0},{4,1},{5,2},{6,3},{7,4},{8,13},{9,14},{10,... | collective-permute-start | bytes 56 | tf_op jit(solution)/shard_map/ppermute | solution.py:245
  5.0 27.3 %collective-permute-start.3 = (s32[4]{0:T(128)}, s32[4]{0:T(128)S(1)}, u32[]{:S(2)}, u32[]{:S(2)}) collective-permute-start(s32[4]{0:T(128)} %param.15), channel_id=1, source_target_pairs={{0,4},{1,5},{2,6},{3,7},{4,0},{5,1},{6,2},{7,3},{8,12},{9,13},{10,... | collective-permute-start | bytes 56 | tf_op jit(solution)/shard_map/ppermute | solution.py:245
  5.3 26.9 %collective-permute-start.2 = (s32[4]{0:T(128)}, s32[4]{0:T(128)S(1)}, u32[]{:S(2)}, u32[]{:S(2)}) collective-permute-start(s32[4]{0:T(128)} %param.15), channel_id=1, source_target_pairs={{0,3},{1,4},{2,5},{3,6},{4,7},{5,0},{6,1},{7,2},{8,11},{9,12},{10,... | collective-permute-start | bytes 56 | tf_op jit(solution)/shard_map/ppermute | solution.py:245
  7.0 25.3 %collective-permute-start.1 = (s32[4]{0:T(128)}, s32[4]{0:T(128)S(1)}, u32[]{:S(2)}, u32[]{:S(2)}) collective-permute-start(s32[4]{0:T(128)} %param.15), channel_id=1, source_target_pairs={{0,2},{1,3},{2,4},{3,5},{4,6},{5,7},{6,0},{7,1},{8,10},{9,11},{10,... | collective-permute-start | bytes 56 | tf_op jit(solution)/shard_map/ppermute | solution.py:245
  9.4 22.8 %collective-permute-start = (s32[4]{0:T(128)}, s32[4]{0:T(128)S(1)}, u32[]{:S(2)}, u32[]{:S(2)}) collective-permute-start(s32[4]{0:T(128)} %param.15), channel_id=1, source_target_pairs={{0,1},{1,2},{2,3},{3,4},{4,5},{5,6},{6,7},{7,0},{8,9},{9,10},{10,1... | collective-permute-start | bytes 56 | tf_op jit(solution)/shard_map/ppermute | solution.py:245
  11.0 0.7 %copy-start.7 = (bf16[512]{0:T(512)(128)(2,1)S(1)}, bf16[512]{0:T(512)(128)(2,1)}, u32[]{:S(2)}) copy-start(bf16[512]{0:T(512)(128)(2,1)} %ground_hbm.1) | copy-start | bytes 3076
  11.0 0.7 %copy-start.5 = (s32[512]{0:T(512)S(1)}, s32[512]{0:T(512)}, u32[]{:S(2)}) copy-start(s32[512]{0:T(512)} %param.14) | copy-start | bytes 6148
  11.0 0.7 %copy-start.6 = (bf16[512]{0:T(512)(128)(2,1)S(1)}, bf16[512]{0:T(512)(128)(2,1)}, u32[]{:S(2)}) copy-start(bf16[512]{0:T(512)(128)(2,1)} %cosine_hbm.1) | copy-start | bytes 3076
  11.7 0.9 %copy-start = (bf16[7,32,512]{2,1,0:T(8,128)(2,1)S(1)}, bf16[7,32,512]{2,1,0:T(8,128)(2,1)}, u32[]{:S(2)}) copy-start(bf16[7,32,512]{2,1,0:T(8,128)(2,1)} %gases_hbm.1) | copy-start | bytes 688132
  12.6 0.9 %copy-start.1 = (bf16[112,7,60]{0,2,1:T(8,128)(2,1)S(1)}, bf16[112,7,60]{0,2,1:T(8,128)(2,1)}, u32[]{:S(2)}) copy-start(bf16[112,7,60]{0,2,1:T(8,128)(2,1)} %param.16) | copy-start | bytes 282244
  13.5 0.8 %copy-start.2 = (s32[32,512]{1,0:T(8,128)S(1)}, s32[32,512]{1,0:T(8,128)}, u32[]{:S(2)}) copy-start(s32[32,512]{1,0:T(8,128)} %bins_hbm.1) | copy-start | bytes 196612
  14.3 0.7 %copy-start.4 = (bf16[112,60]{0,1:T(8,128)(2,1)S(1)}, bf16[112,60]{0,1:T(8,128)(2,1)}, u32[]{:S(2)}) copy-start(bf16[112,60]{0,1:T(8,128)(2,1)} %param.17) | copy-start | bytes 40324
  28.4 0.7 %copy-start.8 = (s32[4]{0:T(128)S(1)}, s32[4]{0:T(128)}, u32[]{:S(2)}) copy-start(s32[4]{0:T(128)} %param.15) | copy-start | bytes 52
  29.0 4.5 %collective-permute-start.6 = (s32[4]{0:T(128)S(1)}, s32[4]{0:T(128)S(1)}, u32[]{:S(2)}, u32[]{:S(2)}) collective-permute-start(s32[4]{0:T(128)S(1)} %copy-done.8), channel_id=1, source_target_pairs={{0,7},{1,0},{2,1},{3,2},{4,3},{5,4},{6,5},{7,6},{8,15},{9,8},{10,9... | collective-permute-start | bytes 56 | tf_op jit(solution)/shard_map/ppermute | solution.py:245
  32.3 3.5 %collective-permute-start.5 = (s32[4]{0:T(128)S(1)}, s32[4]{0:T(128)S(1)}, u32[]{:S(2)}, u32[]{:S(2)}) collective-permute-start(s32[4]{0:T(128)S(1)} %copy-done.8), channel_id=1, source_target_pairs={{0,6},{1,7},{2,0},{3,1},{4,2},{5,3},{6,4},{7,5},{8,14},{9,15},{10,... | collective-permute-start | bytes 56 | tf_op jit(solution)/shard_map/ppermute | solution.py:245

commit v2 on v1

--- a/solution.py
+++ b/solution.py
@@ -14,6 +14,7 @@
 STEP = 4
 HALVES = 2
 BIN_ROWS = 64
+VMEM_BYTES = 63 * 1024 * 1024
 LOG2E = math.log2(math.e)
 
 
@@ -44,13 +45,12 @@
     copied,
     wide_buf,
     table_ref,
-    scatter_ref,
     gas_buf,
     slope_buf,
-    tau_even,
-    tau_odd,
-    half_even,
-    half_odd,
+    weight_even,
+    weight_odd,
+    optic_even,
+    optic_odd,
     up_buf,
     rise_buf,
     pass_buf,
@@ -61,7 +61,7 @@
     net_buf,
 ):
     gas_count, levels, columns = gases_ref.shape
-    points = table_ref.shape[0]
+    points = table_ref.shape[0] // 2
     half = points // HALVES
     vregs = half // ROWS
     groups = levels // STEP
@@ -96,36 +96,39 @@
     first_row = gas_count * BIN_ROWS
     wide_buf[first_row : first_row + absorb_ref.shape[1], :points] = 0.5 * albedo_ref[...].astype(jnp.float32)
     turned = [
-        jnp.transpose(wide_buf[i * LANES : (i + 1) * LANES])[:points].astype(jnp.bfloat16)
+        jnp.transpose(wide_buf[i * LANES : (i + 1) * LANES])[:points]
         for i in range(wide_buf.shape[0] // LANES)
     ]
     whole = jnp.concatenate(turned, axis=1)
-    table_ref[...] = whole[:, :first_row]
-    scatter_ref[...] = whole[:, first_row : first_row + BIN_ROWS]
+    gas_lane = lax.broadcasted_iota(jnp.int32, whole.shape, 1) < first_row
+    table_ref[:points] = jnp.where(gas_lane, whole, 0.0).astype(jnp.bfloat16)
+    table_ref[points:] = jnp.where(gas_lane, 0.0, whole).astype(jnp.bfloat16)
     for gas in range(gas_count):
         gas_buf[gas] = gases_ref[gas].astype(jnp.float32)
     cosine = jnp.broadcast_to(cosine_ref[...].astype(jnp.float32).reshape(1, columns), (ROWS, columns))
     slope_buf[...] = (-LOG2E) / cosine
 
-    def optical(layer, tile, tau_ref, half_ref, slot):
+    def weigh(layer, tile, weight_ref):
         cols = slice(tile * TILE, (tile + 1) * TILE)
         spread = (BIN_ROWS, TILE)
         bins = jnp.broadcast_to(bins_ref[pl.ds(layer, 1), cols], spread)
         hit = bins == lax.broadcasted_iota(jnp.int32, spread, 0)
         selector = jnp.where(hit, 1.0, 0.0).astype(jnp.bfloat16)
-        parts = []
         for gas in range(gas_count):
             amount = jnp.broadcast_to(gas_buf[gas, pl.ds(layer, 1), cols], (16, TILE)).astype(jnp.bfloat16)
             amount = jnp.concatenate([amount] * (BIN_ROWS // 16), axis=0)
-            parts.append(amount * selector)
-        weighted = jnp.concatenate(parts, axis=0)
-        tau_ref[slot, :, cols] = jnp.dot(table_ref[...], weighted, preferred_element_type=jnp.float32)
-        half_ref[slot, :, cols] = jnp.dot(scatter_ref[...], selector, preferred_element_type=jnp.float32)
-
-    def advance(first, slots, chunk, tau_ref, half_ref):
+            weight_ref[gas * BIN_ROWS : (gas + 1) * BIN_ROWS] = amount * selector
+        weight_ref[gas_count * BIN_ROWS : (gas_count + 1) * BIN_ROWS] = selector
+
+    def optical(slot, tile, weight_ref, optic_ref):
+        cols = slice(tile * TILE, (tile + 1) * TILE)
+        optic_ref[slot, :, cols] = jnp.dot(table_ref[...], weight_ref[...], preferred_element_type=jnp.float32)
+
+    def advance(first, slots, chunk, optic_ref):
         block, part = divmod(chunk, HALVES)
         cols = slice(block * LANES, (block + 1) * LANES)
         rows = slice(part * half, (part + 1) * half)
+        half_rows = slice(points + part * half, points + (part + 1) * half)
         shape = (vregs, ROWS, LANES)
         slope = slope_buf[:, cols]
         refl = refl_buf[rows, cols].reshape(shape)
@@ -133,8 +136,8 @@
         direct = direct_buf[rows, cols].reshape(shape)
         for slot in range(slots):
             layer = first + slot
-            tau = tau_ref[slot, rows, cols].reshape(shape)
-            half_albedo = half_ref[slot, rows, cols].reshape(shape)
+            tau = optic_ref[slot, rows, cols].reshape(shape)
+            half_albedo = optic_ref[slot, half_rows, cols].reshape(shape)
             fading = jnp.exp2(tau * (-1.66 * LOG2E))
             passed = jnp.exp2(tau * slope)
             reflect = half_albedo * (1.0 - fading)
@@ -159,23 +162,33 @@
     for part in range(HALVES):
         gain_buf[part, 0] = cosine * float(vregs)
 
+    chunks = blocks * HALVES
     work = [(slot, tile) for slot in range(STEP) for tile in range(tiles)]
-    for slot, tile in work:
-        optical(slot, tile, tau_even, half_even, slot)
-
-    chunks = blocks * HALVES
+    count = len(work)
+    weights = (weight_even, weight_odd)
+
+    weigh(0, 0, weights[0])
+    for place, (slot, tile) in enumerate(work):
+        after_slot, after_tile = (work + [(STEP, 0)])[place + 1]
+        weigh(after_slot, after_tile, weights[(place + 1) % 2])
+        optical(slot, tile, weights[place % 2], optic_even)
 
     def down_pair(pair, carry):
         first = pair * (2 * STEP)
-        following = jnp.minimum(first + 2 * STEP, levels - STEP)
-        for chunk in range(chunks):
-            for slot, tile in work[chunk * len(work) // chunks:(chunk + 1) * len(work) // chunks]:
-                optical(first + STEP + slot, tile, tau_odd, half_odd, slot)
-            advance(first, STEP, chunk, tau_even, half_even)
-        for chunk in range(chunks):
-            for slot, tile in work[chunk * len(work) // chunks:(chunk + 1) * len(work) // chunks]:
-                optical(following + slot, tile, tau_even, half_even, slot)
-            advance(first + STEP, STEP, chunk, tau_odd, half_odd)
+        tasks = []
+        for back in range(2):
+            tasks += [(first + (back + 1) * STEP, slot, tile, (optic_odd, optic_even)[back]) for slot, tile in work]
+        tasks.append((first + 3 * STEP, 0, 0, None))
+        done = 0
+        for step in range(2 * chunks):
+            while done < (step + 1) * count // chunks:
+                _, slot, tile, optic_ref = tasks[done]
+                after, after_slot, after_tile, _ = tasks[done + 1]
+                weigh(jnp.minimum(after + after_slot, levels - 1), after_tile, weights[(done + 1) % 2])
+                optical(slot, tile, weights[done % 2], optic_ref)
+                done += 1
+            back, chunk = divmod(step, chunks)
+            advance(first + back * STEP, STEP, chunk, (optic_even, optic_odd)[back])
         return carry
 
     lax.fori_loop(0, groups // 2, down_pair, 0)
@@ -241,12 +254,11 @@
     me = lax.axis_index("span")
     gas_count, levels, columns = gases.shape
     points, _, bins = absorption.shape
-    ring = [
-        lax.ppermute(sunlit, "span", [(i, (i + hop) % group_size) for i in range(group_size)])
-        for hop in range(1, group_size)
-    ]
+    tile = jnp.broadcast_to(jnp.pad(sunlit, (0, LANES - sunlit.shape[0]))[None], (ROWS, LANES))
+    gathered = lax.all_gather(tile, "span", axis=0, tiled=True).reshape(group_size, ROWS, LANES)
     field = pltpu.VMEM((levels, points, columns), jnp.float32)
-    staged = pltpu.VMEM((STEP, points, columns), jnp.float32)
+    staged = pltpu.VMEM((STEP, 2 * points, columns), jnp.float32)
+    weight = pltpu.VMEM(((gas_count + 1) * BIN_ROWS, TILE), jnp.bfloat16)
     state = pltpu.VMEM((points, columns), jnp.float32)
     heat, owner = pl.pallas_call(
         functools.partial(heating_kernel, columns // group_size),
@@ -267,12 +279,11 @@
             pltpu.VMEM((bins, points), scattering.dtype),
             pltpu.SemaphoreType.DMA((8,)),
             pltpu.VMEM((-(-(gas_count + 1) * BIN_ROWS // LANES) * LANES, LANES), jnp.float32),
-            pltpu.VMEM((points, gas_count * BIN_ROWS), jnp.bfloat16),
-            pltpu.VMEM((points, BIN_ROWS), jnp.bfloat16),
+            pltpu.VMEM((2 * points, (gas_count + 1) * BIN_ROWS), jnp.bfloat16),
             pltpu.VMEM(gases.shape, jnp.float32),
             pltpu.VMEM((ROWS, columns), jnp.float32),
-            staged,
-            staged,
+            weight,
+            weight,
             staged,
             staged,
             field,
@@ -284,7 +295,7 @@
             pltpu.VMEM((HALVES, levels + 1, ROWS, columns), jnp.float32),
             pltpu.VMEM((levels + 1, ROWS, columns), jnp.float32),
         ],
-        compiler_params=pltpu.CompilerParams(vmem_limit_bytes=48 * 1024 * 1024),
+        compiler_params=pltpu.CompilerParams(vmem_limit_bytes=VMEM_BYTES),
         cost_estimate=pl.CostEstimate(
             flops=40 * levels * points * columns, bytes_accessed=1 << 20, transcendentals=3 * levels * points * columns
         ),
@@ -299,9 +310,9 @@
         jnp.transpose(scattering),
     )
     place = me * (columns // group_size) // (columns // sunlit.shape[0])
-    flags = lax.dynamic_index_in_dim(jnp.stack([sunlit] + ring), place, axis=1, keepdims=False)
-    hops = lax.rem(me - owner[0] + group_size, group_size)
-    lit = jnp.sum(jnp.where(hops[None] == jnp.arange(group_size, dtype=jnp.int32)[:, None], flags[:, None], 0), axis=0)
+    flags = lax.dynamic_index_in_dim(gathered[:, 0], place, axis=1, keepdims=False)
+    peers = jnp.arange(group_size, dtype=jnp.int32)[:, None]
+    lit = jnp.sum(jnp.where(owner[0][None] == peers, flags[:, None], 0), axis=0)
     return heat * lit.astype(jnp.float32)
 
 

time: 37 us -> 51.7 us (1.40)
  blocking collectives: 0 us -> 32.2 us
  starting transfers between devices: 14.2 us -> 0 us
  waiting for transfers between devices: 3.52 us -> 0 us
  local copies, waits for them, and re-layouts: 4.94 us -> 1.69 us
  Pallas kernels: 13.3 us -> 16 us
  other arithmetic: 0.75 us -> 1.57 us
    all_gather x0 -> x1, blocking collectives: none -> 32.2 us  [local(): lax.all_gather(tile, 'span', axis=0, tiled=True)]
    ppermute x7 -> x0, starting transfers between devices: 14.2 us -> none  [local(): lax.ppermute(sunlit, 'span', [(i, (i + hop) % group_size) for i in range(...]
    unnamed x18 -> x2, local copies, waits for them, and re-layouts: 4.73 us -> 0.65 us
    ppermute x7 -> x0, waiting for transfers between devices: 3.52 us -> none  [local(): lax.ppermute(sunlit, 'span', [(i, (i + hop) % group_size) for i in range(...]
    pallas_call x1, Pallas kernels: 13.3 us -> 16 us  [local(): pl.pallas_call(functools.partial(heating_kernel, columns // group_size),...]
    mul x1, other arithmetic: 0.64 us -> 1.47 us  [local(): return heat * lit.astype(jnp.float32)]
    slice x0 -> x2, local copies, waits for them, and re-layouts: none -> 0.72 us  [the longest x1 0.72 us: local(): lit = jnp.sum(jnp.where(owner[0][None] == peers, flags[:, None], 0), axis=0)]
  transfers between devices with their start and end apart: 7 -> 0, of which waited for: 2 -> 0; matrix products, arithmetic and copies ran while one was open for 0% -> 0% of each run, Pallas kernels for 36% -> 0%
where the time goes in v2:
time: 51.7 us; the launch traced here: 51.5 us
  blocking collectives  32.2 us (62%)
  Pallas kernels  16 us (31%)
  local copies, waits for them, and re-layouts  1.69 us (3%)
  other arithmetic  1.57 us (3%)
    all_gather x1, blocking collectives, local(): lax.all_gather(tile, 'span', axis=0, tiled=True)  32.2 us
    pallas_call x1, Pallas kernels, local(): pl.pallas_call(functools.partial(heating_kernel, columns // group_size),...  16 us
    mul x1, other arithmetic, local(): return heat * lit.astype(jnp.float32)  1.47 us

profile of v2, /device:TPU:0, one launch (start us, length us, event | category | flops | bytes accessed | tf_op | source)
XLA Modules:
  0.0 51.5 jit_solution(16316505833130991452)
XLA Ops:
  0.0 0.0 copy-start
  0.0 0.7 %copy-done = s32[4]{0:T(128)S(1)} copy-done((s32[4]{0:T(128)S(1)}, s32[4]{0:T(128)}, u32[]{:S(2)}) %copy-start) | copy-done | bytes 40
  0.7 32.2 %all_gather.3 = s32[64,128]{1,0:T(8,128)S(1)} all-gather(s32[8,128]{1,0:T(8,128)S(1)} %broadcast_in_dim.23), channel_id=1, replica_groups=mesh['band'=4,'span'=8] {'span'}, dimensions={0}, use_global_device_ids=true | all-gather | bytes 36864 | tf_op jit(solution)/shard_map/all_gather | solution.py:258
  32.9 0.3 dynamic-slice_reduce_fusion
  33.2 16.0 %shard_map.91 = (f32[32,512]{1,0:T(8,128)}, s32[8,512]{1,0:T(8,128)}) custom-call(bf16[7,32,512]{2,1,0:T(8,128)(2,1)} %gases_hbm.1, s32[32,512]{1,0:T(8,128)} %bins_hbm.1, bf16[32,512]{1,0:T(8,128)(2,1)} %mass_hbm.1, bf16[512]{0:T(512)(128)(2,1)} %cosine_hbm.1, bf16[512]{0:T(512)(128)(2,1)} %ground_hbm.1, s32[1,512]{1,0:T(1,128)} %bitcast.9, ...), custom_call_target="tpu_custom_call" | custom-call | flops 73400320 | bytes 1048576 | tf_op jit(solution)/shard_map/pallas_call | solution.py:263
  49.2 0.7 %slice.6 = s32[1,512]{1,0:T(1,128)S(1)} slice(s32[8,512]{1,0:T(8,128)} %get-tuple-element.8), slice={[0:1], [0:512]} | slice | bytes 4096 | tf_op jit(solution)/shard_map/slice | solution.py:315
  49.9 0.1 select_reduce_fusion
  50.0 1.5 %broadcast_multiply_fusion = f32[32,512]{1,0:T(8,128)} fusion(f32[32,512]{1,0:T(8,128)} %get-tuple-element.7, f32[512]{0:T(512)S(1)} %convert_element_type.7), kind=kLoop, calls=%fused_computation | loop fusion | flops 16384 | bytes 133120 | tf_op jit(solution)/shard_map/mul | solution.py:316
  (4 shorter events, 0.0 us)
Async XLA Ops:
  0.0 0.7 %copy-start = (s32[4]{0:T(128)S(1)}, s32[4]{0:T(128)}, u32[]{:S(2)}) copy-start(s32[4]{0:T(128)} %param.15) | copy-start | bytes 52
